TPU v7x, 512 devices: a whole 4x4x16 slice. The times are simulated.
512 devices in a mesh: dp: 2 (over core), space: 32 (over y, z_hi, x), filter: 8 (over z_lo).
Axes of the slice: x: 4, y: 4, z: 16 (z_hi: 2, z_lo: 8; z = z_hi * 8 + z_lo), core: 2. Of those that a mesh axis runs over, the one named last changes fastest.
Arguments:
- volumes: bfloat16 [2, 256, 32, 512], P('dp', 'filter', 'space'), may hold values from -6 to 6
- weight: bfloat16 [27, 256, 256], P(None, 'filter'), may hold values from -0.078125 to 0.078125
- bias: float32 [256], P('filter'), may hold values from -3 to 3
- cotangent: bfloat16 [2, 256, 32, 512], P('dp', 'filter', 'space'), may hold values from -6 to 6
Outputs:
- activations: bfloat16 [2, 256, 32, 512], P('dp', 'filter', 'space')
- grad_input: bfloat16 [2, 256, 32, 512], P('dp', 'filter', 'space')
- grad_weight: float32 [27, 256, 256], P(None, 'filter')
- grad_bias: float32 [256], P('filter')
All inputs are finite; a program needn't handle non-finite values.
Results may differ from a plain program's by a relative error of at most 0.0075.
Values may be sent and summed in bfloat16 or wider, within the bound.
A program may use at most 64 MiB of HBM per device.

v0:
```python
import math

import jax
import jax.numpy as jnp
from jax import lax
from jax.sharding import PartitionSpec as P

HEIGHT = 16
BREADTH = 32


plane_steps = [(-1, -1), (-1, 0), (-1, 1), (0, -1), (0, 0), (0, 1), (1, -1), (1, 0), (1, 1)]


def padded_2(cells, sides, width):
    for axis, dim in sides:
        count = lax.axis_size(axis)
        ends = count - 1
        head = lax.slice_in_dim(cells, 0, width, axis=dim)
        tail = lax.slice_in_dim(cells, cells.shape[dim] - width, cells.shape[dim], axis=dim)
        cells = jnp.concatenate(
            [
                lax.ppermute(tail, axis, [(i, (i + 1) % count) for i in range(ends)]),
                cells,
                lax.ppermute(head, axis, [((i + 1) % count, i) for i in range(ends)]),
            ],
            axis=dim,
        )
    return cells


def shift_plane(block, step_row, step_col):
    face_len = HEIGHT * BREADTH
    margin = BREADTH + 1
    widths = [(0, 0)] * (block.ndim - 1) + [(margin, margin)]
    padded = jnp.pad(block, widths)
    offset = step_row * BREADTH + step_col
    moved = lax.slice_in_dim(
        padded, margin + offset, margin + offset + face_len, axis=block.ndim - 1
    )
    position = jnp.arange(face_len, dtype=jnp.int32)
    row_index = position // BREADTH + step_row
    col_index = position % BREADTH + step_col
    inside = (row_index >= 0) & (row_index < HEIGHT) & (col_index >= 0) & (col_index < BREADTH)
    return moved * inside.astype(block.dtype)


def tap_products(padded, grouped_rows, starts, direction):
    planes = padded.shape[1] - 2
    face_len = padded.shape[2]
    count = grouped_rows.shape[2]
    flat = padded.reshape(padded.shape[0], (planes + 2) * face_len)
    total = jnp.zeros((count, planes, face_len), jnp.float32)
    for index, (step_row, step_col) in enumerate(plane_steps):
        taps = grouped_rows[:, index].reshape(3 * count, grouped_rows.shape[3])
        product = jnp.dot(taps, flat, preferred_element_type=jnp.float32).reshape(
            3, count, planes + 2, face_len
        )
        summed = product[0, :, starts[0] : starts[0] + planes]
        summed = summed + product[1, :, starts[1] : starts[1] + planes]
        summed = summed + product[2, :, starts[2] : starts[2] + planes]
        total = total + shift_plane(summed, direction * step_row, direction * step_col)
    return total.reshape(count, planes * face_len)


def forward_terms(padded, weight):
    grouped = weight.reshape(3, 9, weight.shape[1], weight.shape[2])
    return tap_products(padded, grouped, (0, 1, 2), 1)


def weight_terms(padded, grad):
    planes = padded.shape[1] - 2
    face_len = padded.shape[2]
    count = grad.shape[0]
    flat = padded.reshape(padded.shape[0], (planes + 2) * face_len)
    grad_planes = grad.reshape(count, planes, face_len)
    parts = []
    for step_row, step_col in plane_steps:
        moved = shift_plane(grad_planes, -step_row, -step_col)
        placed = jnp.stack(
            [jnp.pad(moved, ((0, 0), (1 + depth, 1 - depth), (0, 0))) for depth in (-1, 0, 1)]
        )
        placed = placed.reshape(3 * count, (planes + 2) * face_len)
        term = lax.dot_general(
            placed, flat, (((1,), (1,)), ((), ())), preferred_element_type=jnp.float32
        )
        parts.append(term.reshape(3, count, padded.shape[0]))
    joined = jnp.stack(parts, axis=1)
    return joined.reshape(27, count, padded.shape[0])


def per_device(volumes, weight, bias, cotangent):
    planes = volumes.shape[2]
    face_len = volumes.shape[3]
    rows = weight.shape[1]
    padded_local = padded_2(volumes, (("space", 2),), 1)
    padded = lax.all_gather(padded_local, "filter", axis=1, tiled=True)[0]
    pre = forward_terms(padded, weight) + bias[:, None]
    sig = jax.nn.sigmoid(pre)
    activations = (pre * sig).astype(jnp.bfloat16).reshape(1, rows, planes, face_len)
    upstream = cotangent[0].reshape(rows, planes * face_len).astype(jnp.float32)
    grad = (upstream * sig * (1.0 + pre * (1.0 - sig))).astype(jnp.bfloat16)
    weight_part = weight_terms(padded, grad)
    bias_part = jnp.sum(grad.astype(jnp.float32), axis=1)
    grad_local = padded_2(grad.reshape(1, rows, planes, face_len), (("space", 2),), 1)
    full_weight = lax.all_gather(weight, "filter", axis=1, tiled=True)
    full_grad = lax.all_gather(grad_local, "filter", axis=1, tiled=True)[0]
    first = lax.axis_index("filter") * rows
    slab = lax.dynamic_slice_in_dim(full_weight, first, rows, 2)
    flipped = jnp.transpose(slab, (0, 2, 1)).reshape(3, 9, rows, slab.shape[1])
    grad_input = tap_products(full_grad, flipped, (2, 1, 0), -1)
    weight_sum, bias_sum = lax.psum((weight_part, bias_part), ("dp", "space"))
    scale = 1.0 / math.sqrt(lax.axis_size("dp") * lax.axis_size("space") * planes * face_len)
    grad_input = grad_input.astype(jnp.bfloat16).reshape(1, rows, planes, face_len)
    return (activations, grad_input, weight_sum * scale, bias_sum * scale)


def solution(mesh):
    return jax.shard_map(
        per_device,
        mesh=mesh,
        in_specs=(
            P("dp", "filter", "space", None),
            P(None, "filter", None),
            P("filter"),
            P("dp", "filter", "space", None),
        ),
        out_specs=(
            P("dp", "filter", "space", None),
            P("dp", "filter", "space", None),
            P(None, "filter", None),
            P("filter"),
        ),
        check_vma=False,
    )
```

profile of v0, /device:TPU:1, one launch (start us, length us, event | category | flops | bytes accessed | tf_op | source)
XLA Modules:
  0.0 1241.3 jit_solution(18098395640378375201)
XLA Ops:
  8.0 3.9 collective-permute-start
  12.0 1.3 collective-permute-start.1
  13.3 0.6 fusion.171
  13.9 0.6 fusion.168
  14.5 0.6 fusion.164
  15.1 0.6 fusion.158
  15.7 0.6 fusion.154
  16.3 0.6 fusion.167
  16.9 0.6 fusion.163
  17.4 0.6 fusion.159
  18.0 0.6 fusion.155
  18.6 1.7 fusion.192
  20.3 0.6 fusion.162
  20.9 0.8 pad_maximum_fusion
  21.6 47.8 %all_gather.9 = bf16[1,256,3,512]{3,1,2,0:T(8,128)(2,1)S(1)} all-gather(bf16[1,32,3,512]{3,1,2,0:T(8,128)(2,1)S(1)} %pad_maximum_fusion), channel_id=1, replica_groups=mesh['dp'=2,'space'=32,'filter'=8] {'filter'}, dimensions={1}, use_global_device_ids=true | all-gather | bytes 884736 | tf_op jit(solution)/shard_map/all_gather | solution.py:97
  69.7 0.4 convolution_bitcast_fusion
  70.1 0.4 reshape.1142
  70.7 0.4 convolution_bitcast_fusion.1
  71.1 0.4 reshape.1141
  71.7 0.4 convolution_bitcast_fusion.2
  72.1 0.4 reshape.1140
  72.7 0.4 convolution_bitcast_fusion.3
  73.1 0.4 reshape.1139
  74.1 0.4 reshape.1138
  74.7 0.4 convolution_bitcast_fusion.5
  75.1 0.4 reshape.1137
  75.7 1.2 convolution_bitcast_fusion.6
  76.9 0.4 reshape.1136
  77.3 0.8 fusion.185
  78.2 1.2 convolution_bitcast_fusion.7
  79.3 0.4 reshape.1135
  79.8 0.8 fusion.184
  81.1 0.4 reshape.1134
  81.9 0.9 fusion.129
  82.7 0.9 fusion.131
  83.8 0.9 convert_reduce_fusion
  84.6 0.8 broadcast_multiply_fusion.1
  90.9 0.8 stack.119
  91.7 0.8 stack.121
  92.5 0.8 stack.120
  94.2 0.8 stack.127
  95.8 1.3 fusion.6
  98.7 1.0 copy.189
  99.8 0.5 all-gather.2.cloned.1.call-update
  100.3 0.7 fusion.106
  101.1 1.3 collective-permute-start.3
  102.4 4.0 collective-permute-start.2
  106.4 304.3 %psum.15 = f32[32]{0:T(128)S(1)} all-reduce(f32[32]{0:T(128)S(1)} %copy-done.20), channel_id=1, replica_groups=mesh['dp'=2,'space'=32,'filter'=8] {'dp','space'}, use_global_device_ids=true, to_apply=%region_2.3 | all-reduce | flops 32 | bytes 256 | tf_op jit(solution)/shard_map/psum | solution.py:112
  410.7 0.5 broadcast_multiply_fusion.2
  411.2 45.1 %all_gather.11 = bf16[1,256,3,512]{3,1,2,0:T(8,128)(2,1)S(1)} all-gather(bf16[1,32,3,512]{3,1,2,0:T(8,128)(2,1)S(1)} %pad_maximum_fusion.1), channel_id=1, replica_groups=mesh['dp'=2,'space'=32,'filter'=8] {'filter'}, dimensions={1}, use_global_device_ids=true | all-gather | bytes 884736 | tf_op jit(solution)/shard_map/all_gather | solution.py:107
  456.7 767.8 %all-reduce.46.cloned.1.call-done = f32[27,32,256]{2,1,0:T(8,128)} async-done(((f32[27,32,256]{2,1,0:T(8,128)}), f32[27,32,256]{2,1,0:T(8,128)}) %all-reduce.46.cloned.1.call-update) | async-done | bytes 884752 | tf_op jit(solution)/shard_map/psum | solution.py:112
  1224.5 2.2 broadcast_multiply_fusion
  1226.7 2.0 constant_dynamic-slice_fusion
  1228.7 0.8 copy.244
  1229.5 0.4 fusion.23
  1229.9 0.4 fusion.21
  1230.2 0.4 fusion.19
  1230.6 0.4 fusion.17
  1231.0 0.4 fusion.15
  1231.4 0.4 fusion.13
  1231.7 0.4 fusion.11
  1232.1 0.4 fusion.9
  1232.5 0.4 fusion.25
  1233.0 0.8 fusion.141
  (122 shorter events, 11.6 us)
Async XLA Ops:
  8.0 1216.5 %all-reduce.46.cloned.1.call-start = ((), (), s32[]{:S(2)}) async-start(), calls=%async_computation.1 | async-start | bytes 1769472 | tf_op jit(solution)/shard_map/psum | solution.py:112
  8.0 12.8 %collective-permute-start = (bf16[1,32,1,512]{3,1,2,0:T(8,128)(2,1)}, bf16[1,32,1,512]{3,1,2,0:T(8,128)(2,1)S(1)}, u32[]{:S(2)}, u32[]{:S(2)}) collective-permute-start(bf16[1,32,1,512]{3,1,2,0:T(8,128)(2,1)} %param.4), channel_id=1, source_target_pairs={{0,8},{8,16},{16,24},{24,32},{32,40},{40,48},{48,56},{56,64},{64,7... | collective-permute-start | bytes 98312 | tf_op jit(solution)/shard_map/ppermute | solution.py:23
  12.0 8.9 collective-permute-start.1
  79.3 4.3 copy-start
  81.0 2.7 copy-start.2
  81.0 2.7 copy-start.3
  81.0 2.7 copy-start.4
  81.0 2.7 copy-start.5
  81.0 2.7 copy-start.6
  81.0 2.7 copy-start.7
  81.0 2.7 copy-start.8
  81.0 2.7 copy-start.9
  81.0 2.7 copy-start.10
  81.1 2.7 copy-start.11
  81.1 4.4 copy-start.12
  81.1 4.4 copy-start.13
  81.5 4.0 copy-start.14
  81.5 4.0 copy-start.15
  81.5 4.0 copy-start.16
  81.5 4.0 copy-start.17
  81.6 4.0 copy-start.18
  81.6 4.0 copy-start.19
  95.0 2.4 copy-start.1
  97.9 8.4 copy-start.20
  99.8 1126.9 %all-gather.2.cloned.1.call-start = ((), (), s32[]{:S(2)}) async-start(), calls=%async_computation | async-start | bytes 3981312 | tf_op jit(solution)/shard_map/all_gather | solution.py:106
  101.1 310.1 %collective-permute-start.3 = (bf16[1,32,1,512]{3,1,2,0:T(8,128)(2,1)S(1)}, bf16[1,32,1,512]{3,1,2,0:T(8,128)(2,1)S(1)}, u32[]{:S(2)}, u32[]{:S(2)}) collective-permute-start(bf16[1,32,1,512]{3,1,2,0:T(8,128)(2,1)S(1)} %get-tuple-element.44), channel_id=1, source_target_pairs={{8,0},{16,8},{24,16},{32,24},{40,32},{48,40},{56,48},{64,56},{72,6... | collective-permute-start | bytes 98312 | tf_op jit(solution)/shard_map/ppermute | solution.py:25
  102.4 308.9 %collective-permute-start.2 = (bf16[1,32,1,512]{3,1,2,0:T(8,128)(2,1)S(1)}, bf16[1,32,1,512]{3,1,2,0:T(8,128)(2,1)S(1)}, u32[]{:S(2)}, u32[]{:S(2)}) collective-permute-start(bf16[1,32,1,512]{3,1,2,0:T(8,128)(2,1)S(1)} %get-tuple-element.44), channel_id=1, source_target_pairs={{0,8},{8,16},{16,24},{24,32},{32,40},{40,48},{48,56},{56,64},{64,7... | collective-permute-start | bytes 98312 | tf_op jit(solution)/shard_map/ppermute | solution.py:23
Sparse Core Ops, SparseCore 0:
  99.9 1124.5 all-reduce.45
Sparse Core Ops, SparseCore 1:
  102.3 115.2 all-gather.1
where the time goes:
time: 1240 us
  waiting for transfers between devices  768 us (62%)
  blocking collectives  397 us (32%)
  local copies, waits for them, and re-layouts  22.4 us (2%)
  between operations  16.3 us (1%)
  other arithmetic  14.7 us (1%)
    psum x1, waiting for transfers between devices, per_device(): weight_sum, bias_sum = lax.psum((weight_part, bias_part), ('dp', 'space'))  768 us
    psum x1, blocking collectives, per_device(): weight_sum, bias_sum = lax.psum((weight_part, bias_part), ('dp', 'space'))  304 us
    all_gather x1, blocking collectives, per_device(): padded = lax.all_gather(padded_local, 'filter', axis=1, tiled=True)[0]  47.8 us
    all_gather x1, blocking collectives, per_device(): full_grad = lax.all_gather(grad_local, 'filter', axis=1, tiled=True)[0]  45.1 us
  transfers between devices with their start and end apart: 6, of which 1 were waited for; matrix products, arithmetic and copies ran while one was open for 1% of the time, Pallas kernels for 0%

commit v1 on v0

v1 whole, which is shorter than its diff:
```python
import functools
import math

import jax
import jax.numpy as jnp
from jax import lax
from jax.experimental import pallas as pl
from jax.experimental.pallas import tpu as pltpu
from jax.sharding import PartitionSpec as P

HEIGHT = 16
BREADTH = 32
FACE = HEIGHT * BREADTH
ROWS = 32
CHANNELS = 256
TAPS = 27
UNITS = 28
OWNERS = UNITS // 2
MESH = pl.DeviceIdType.MESH
F32 = jnp.float32
BF16 = jnp.bfloat16
SHIFTS = [(b, c) for b in (-1, 0, 1) for c in (-1, 0, 1)]


def masks():
    f = lax.broadcasted_iota(jnp.int32, (ROWS, FACE), 1)
    row, col = f // BREADTH, f % BREADTH
    row_ok = {b: (row + b >= 0) & (row + b < HEIGHT) for b in (-1, 1)}
    col_ok = {c: (col + c >= 0) & (col + c < BREADTH) for c in (-1, 1)}
    return row_ok, col_ok


def pull(x, amount, ok):
    return jnp.where(ok, pltpu.roll(x, (-amount) % FACE, 1), 0.0)


def pack(v):
    high = v.astype(BF16).astype(F32)
    low = v - high
    row = lax.broadcasted_iota(jnp.int32, (16, CHANNELS), 0)
    return jnp.where(row == 0, high, jnp.where(row == 1, low, 0.0)).astype(BF16)


def unpack(unit):
    u = unit.astype(F32)
    row = lax.broadcasted_iota(jnp.int32, u.shape, 0)
    return jnp.sum(jnp.where(row < 2, u, 0.0), axis=0, keepdims=True)


def kernel(
    scale,
    vol, w, bias, cot,
    act_o, gin_o, gw_o, gb_o,
    V, COT, QS, QR, Q0, ACT, GN, GS, Fp, S, R0, T1, R1, O, N, RG,
    z_send, z_recv, c_sem, q_send, q_recv, g_send, g_recv,
    d_sem, rs_send, rs_recv, ag_send, ag_recv, e_sem, n_send, n_recv,
):
    d = lax.axis_index("dp")
    s = lax.axis_index("space")
    f = lax.axis_index("filter")
    y = s // 8
    zh = (s // 4) % 2
    x = s % 4
    z = zh * 8 + f
    me = y * 4 + x

    def at_z(k):
        return (d, y * 8 + (k // 8) * 4 + x, k % 8)

    def at_xy(j):
        return (d, (j // 4) * 8 + zh * 4 + j % 4, f)

    def near(k):
        return (z + k + 16) % 16

    other = (1 - d, s, f)

    def copy(src, dst, send, recv, to):
        return pltpu.make_async_remote_copy(
            src_ref=src, dst_ref=dst, send_sem=send, recv_sem=recv,
            device_id=to, device_id_type=MESH,
        )

    barrier = pltpu.get_barrier_semaphore()
    for k in range(1, 16):
        pl.semaphore_signal(barrier, inc=1, device_id=at_z((z + k) % 16), device_id_type=MESH)
        pl.semaphore_signal(barrier, inc=1, device_id=at_xy((me + k) % 16), device_id_type=MESH)
    pl.semaphore_signal(barrier, inc=1, device_id=other, device_id_type=MESH)
    pl.semaphore_wait(barrier, 31)

    even = z % 2 == 0
    step2 = jnp.where(even, 2, -2)
    nears = [near(1), near(-1), (z + step2 + 16) % 16]
    fars = [near(4), near(-4), near(8)]
    V[z] = vol[...]
    COT[zh] = cot[...]
    sends = []

    def shard(slot, to, i):
        c = copy(V.at[slot], V.at[slot], z_send.at[i], z_recv.at[slot], at_z(to))
        c.start()
        sends.append(c)

    def shard_wait(slot):
        copy(V.at[slot], V.at[slot], z_send.at[0], z_recv.at[slot], at_z(nears[0])).wait_recv()

    for i, to in enumerate(fars + nears):
        shard(z, to, i)
    for j, slot in enumerate(fars):
        shard_wait(slot)
        for i, to in enumerate(nears):
            shard(slot, to, 6 + 3 * j + i)
    cot_copy = copy(COT.at[zh], COT.at[zh], c_sem.at[0], c_sem.at[1], at_z(near(8)))
    cot_copy.start()
    sources = [near(1), near(-1), (z - step2 + 16) % 16]
    for far in (0, 4, -4, 8):
        for source in sources:
            shard_wait((source + far + 16) % 16)

    row_ok, col_ok = masks()

    def contribution(p, a):
        plane = V[8 * p : 8 * p + 8].reshape(CHANNELS, FACE)
        taps = w[(a + 1) * 9 * ROWS : (a + 2) * 9 * ROWS, :]
        prod = jnp.dot(taps, plane, preferred_element_type=F32)
        total = None
        for c in (0, -1, 1):
            part = None
            for b in (0, -1, 1):
                i = 3 * (b + 1) + (c + 1)
                term = prod[i * ROWS : (i + 1) * ROWS]
                if b:
                    term = pull(term, BREADTH * b, row_ok[b])
                part = term if part is None else part + term
            if c:
                part = pull(part, c, col_ok[c])
            total = part if total is None else total + part
        return total

    def after(p):
        last = x == 3
        x2 = (x + 1) % 4
        y2 = (y + jnp.where(last, p, 0)) % 4
        return y2 * 4 + x2, jnp.where(last, 1 - p, p)

    def before(p):
        first = x == 0
        x2 = (x + 3) % 4
        y2 = (y + 4 - jnp.where(first, 1 - p, 0)) % 4
        return y2 * 4 + x2, jnp.where(first, 1 - p, p)

    q_copies = []
    for p in (0, 1):
        for side, a, where in ((0, -1, after), (1, 1, before)):
            QS[p, side] = contribution(p, a).astype(BF16)
            j, q = where(p)
            c = copy(QS.at[p, side], QR.at[q, side], q_send.at[p, side], q_recv.at[q, side], at_xy(j))
            c.start()
            q_copies.append(c)
    for p in (0, 1):
        Q0[p] = contribution(p, 0)
    eye = lax.broadcasted_iota(jnp.int32, (ROWS, ROWS), 0) == lax.broadcasted_iota(
        jnp.int32, (ROWS, ROWS), 1
    )
    column = jnp.sum(jnp.where(eye, bias[...], 0.0), axis=1, keepdims=True)
    first_plane = (y == 0) & (x == 0)
    last_plane = (y == 3) & (x == 3)
    cot_copy.wait_recv()
    g_copies = []
    bias_total = jnp.zeros((ROWS, 1), F32)
    for p in (0, 1):
        for side in (0, 1):
            copy(
                QS.at[p, side], QR.at[p, side], q_send.at[p, side], q_recv.at[p, side], other
            ).wait_recv()
        before_term = QR[p, 0].astype(F32)
        after_term = QR[p, 1].astype(F32)
        if p == 0:
            before_term = jnp.where(first_plane, 0.0, before_term)
        else:
            after_term = jnp.where(last_plane, 0.0, after_term)
        pre = Q0[p] + before_term + after_term + column
        sig = jax.nn.sigmoid(pre)
        grad = (COT[p].astype(F32) * sig * (1.0 + pre * (1.0 - sig))).astype(BF16)
        GN[p, 1] = grad
        for side, slot, where in ((0, 2, after), (1, 0, before)):
            j, q = where(p)
            c = copy(GN.at[p, 1], GN.at[q, slot], g_send.at[p, side], g_recv.at[q, side], at_xy(j))
            c.start()
            g_copies.append(c)
        ACT[p] = (pre * sig).astype(BF16)
        bias_total = bias_total + jnp.sum(grad.astype(F32), axis=1, keepdims=True)
    act_o[...] = ACT[zh]

    def shifted(p, a):
        grad = GN[p, a + 1].astype(F32)
        if p == 0 and a == 1:
            grad = jnp.where(first_plane, 0.0, grad)
        if p == 1 and a == -1:
            grad = jnp.where(last_plane, 0.0, grad)
        for c in (-1, 0, 1):
            moved = pull(grad, -c, col_ok[-c]) if c else grad
            for b in (-1, 0, 1):
                t = 9 * (a + 1) + 3 * (b + 1) + (c + 1)
                term = pull(moved, -BREADTH * b, row_ok[-b]) if b else moved
                GS[p, t * ROWS : (t + 1) * ROWS, :] = term.astype(BF16)

    def weight_grad(a):
        rows = slice((a + 1) * 9 * ROWS, (a + 2) * 9 * ROWS)
        total = None
        for p in (0, 1):
            plane = V[8 * p : 8 * p + 8].reshape(CHANNELS, FACE)
            term = lax.dot_general(
                GS[p, rows, :], plane, (((1,), (1,)), ((), ())), preferred_element_type=F32
            )
            total = term if total is None else total + term
        for i in range(9):
            t = 9 * (a + 1) + i
            for h in (0, 1):
                piece = total[i * ROWS + h * 16 : i * ROWS + (h + 1) * 16]
                Fp[h, t] = piece
                S[h, t] = piece.astype(BF16)

    for p in (0, 1):
        shifted(p, 0)
    weight_grad(0)
    eye = lax.broadcasted_iota(jnp.int32, (ROWS, CHANNELS), 0) == lax.broadcasted_iota(
        jnp.int32, (ROWS, CHANNELS), 1
    )
    bias_row = jnp.sum(jnp.where(eye, bias_total, 0.0), axis=0, keepdims=True)
    for h in (0, 1):
        Fp[h, TAPS] = jnp.broadcast_to(bias_row, (16, CHANNELS))
        S[h, TAPS] = pack(bias_row)
    for p in (0, 1):
        for side, slot in ((0, 2), (1, 0)):
            copy(
                GN.at[p, 1], GN.at[p, slot], g_send.at[p, side], g_recv.at[p, side], other
            ).wait_recv()
    for a in (-1, 1):
        for p in (0, 1):
            shifted(p, a)
        weight_grad(a)

    d_copy = copy(S.at[1 - d], R0, d_sem.at[0], d_sem.at[1], other)
    d_copy.start()

    part = lax.dot_general(
        w[...], GS[zh], (((0,), (0,)), ((), ())), preferred_element_type=F32
    )
    for i in range(8):
        N[i] = part[i * ROWS : (i + 1) * ROWS].astype(BF16)
    n_copies = []
    for k in range(1, 8):
        to = (f + k) % 8
        c = copy(N.at[to], RG.at[f], n_send.at[k], n_recv.at[f], (d, s, to))
        c.start()
        n_copies.append(c)

    d_copy.wait_recv()
    summed = Fp[d] + R0[...].astype(F32)
    T1[...] = summed.astype(BF16)
    T1[TAPS] = pack(Fp[d, TAPS, 0:1, :] + unpack(R0[TAPS]))

    def mine(ref, j):
        return ref.at[pl.ds(2 * j, 2)]

    def rs_copy(k):
        to = (me + k) % 16
        return to, copy(mine(T1, to), mine(R1, me), rs_send.at[k], rs_recv.at[me], at_xy(to))

    for k in range(1, 16):
        to, c = rs_copy(k)
        pl.when(to < OWNERS)(c.start)

    @pl.when(me < OWNERS)
    def _():
        R1[pl.ds(2 * me, 2)] = T1[pl.ds(2 * me, 2)]
        for k in range(1, 16):
            source = (me + k) % 16
            copy(
                mine(T1, me), mine(R1, source), rs_send.at[k], rs_recv.at[source], at_xy(source)
            ).wait_recv()
        total = R1[0:2].astype(F32)
        for i in range(1, 16):
            total = total + R1[2 * i : 2 * i + 2].astype(F32)
        O[d, pl.ds(2 * me, 2)] = total.astype(BF16)

        @pl.when(me == OWNERS - 1)
        def _():
            O[d, TAPS] = pack(jnp.sum(total[1, 0:2], axis=0, keepdims=True))

        for k in range(1, 16):
            to = (me + k) % 16
            copy(
                O.at[d, pl.ds(2 * me, 2)], O.at[d, pl.ds(2 * me, 2)],
                ag_send.at[k], ag_recv.at[me], at_xy(to),
            ).start()

    own = N[f].astype(F32)
    for k in range(1, 8):
        source = (f + k) % 8
        copy(N.at[source], RG.at[source], n_send.at[k], n_recv.at[source], (d, s, source)).wait_recv()
        own = own + RG[source].astype(F32)
    gin_o[...] = own.astype(BF16)

    for k in range(1, 16):
        source = (me + k) % 16

        @pl.when(source < OWNERS)
        def _():
            copy(
                O.at[d, pl.ds(2 * source, 2)], O.at[d, pl.ds(2 * source, 2)],
                ag_send.at[k], ag_recv.at[source], at_xy(source),
            ).wait_recv()

    e_copy = copy(O.at[d], O.at[d], e_sem.at[0], e_sem.at[1], other)
    e_copy.start()

    def finish(h):
        gw_o[:, pl.ds(pl.multiple_of(h * 16, 16), 16), :] = O[h, 0:TAPS].astype(F32) * scale

    finish(d)
    copy(O.at[1 - d], O.at[1 - d], e_sem.at[0], e_sem.at[1], other).wait_recv()
    finish(1 - d)
    gb_o[...] = unpack(O[0, TAPS])[:, :128] * scale

    for c in sends + q_copies + g_copies + n_copies + [cot_copy, d_copy, e_copy]:
        c.wait_send()
    for k in range(1, 16):
        to, c = rs_copy(k)
        pl.when(to < OWNERS)(c.wait_send)

    @pl.when(me < OWNERS)
    def _():
        for k in range(1, 16):
            to = (me + k) % 16
            copy(
                O.at[d, pl.ds(2 * me, 2)], O.at[d, pl.ds(2 * me, 2)],
                ag_send.at[k], ag_recv.at[me], at_xy(to),
            ).wait_send()


def per_device(scale, volumes, weight, bias, cotangent):
    vmem = pl.BlockSpec(memory_space=pltpu.VMEM)
    dma = pltpu.SemaphoreType.DMA
    act, gin, gw, gb = pl.pallas_call(
        functools.partial(kernel, scale),
        out_shape=[
            jax.ShapeDtypeStruct((ROWS, FACE), BF16),
            jax.ShapeDtypeStruct((ROWS, FACE), BF16),
            jax.ShapeDtypeStruct((TAPS, ROWS, CHANNELS), F32),
            jax.ShapeDtypeStruct((1, 128), F32),
        ],
        in_specs=[vmem] * 4,
        out_specs=[vmem] * 4,
        scratch_shapes=[
            pltpu.VMEM((16, ROWS, FACE), BF16),
            pltpu.VMEM((2, ROWS, FACE), BF16),
            pltpu.VMEM((2, 2, ROWS, FACE), BF16),
            pltpu.VMEM((2, 2, ROWS, FACE), BF16),
            pltpu.VMEM((2, ROWS, FACE), F32),
            pltpu.VMEM((2, ROWS, FACE), BF16),
            pltpu.VMEM((2, 3, ROWS, FACE), BF16),
            pltpu.VMEM((2, TAPS * ROWS, FACE), BF16),
            pltpu.VMEM((2, UNITS, 16, CHANNELS), F32),
            pltpu.VMEM((2, UNITS, 16, CHANNELS), BF16),
            pltpu.VMEM((UNITS, 16, CHANNELS), BF16),
            pltpu.VMEM((UNITS, 16, CHANNELS), BF16),
            pltpu.VMEM((32, 16, CHANNELS), BF16),
            pltpu.VMEM((2, UNITS, 16, CHANNELS), BF16),
            pltpu.VMEM((8, ROWS, FACE), BF16),
            pltpu.VMEM((8, ROWS, FACE), BF16),
            dma((15,)), dma((16,)), dma((2,)),
            dma((2, 2)), dma((2, 2)), dma((2, 2)), dma((2, 2)),
            dma((2,)), dma((16,)), dma((16,)), dma((16,)), dma((16,)), dma((2,)),
            dma((8,)), dma((8,)),
        ],
        compiler_params=pltpu.CompilerParams(
            collective_id=0, has_side_effects=True, vmem_limit_bytes=48 * 2**20
        ),
    )(
        volumes.reshape(ROWS, FACE),
        weight.reshape(TAPS * ROWS, CHANNELS),
        bias.reshape(1, ROWS),
        cotangent.reshape(ROWS, FACE),
    )
    shape = (1, ROWS, 1, FACE)
    return act.reshape(shape), gin.reshape(shape), gw, gb[0, :ROWS]


def solution(mesh):
    scale = 1.0 / math.sqrt(2 * 32 * FACE)
    return jax.shard_map(
        functools.partial(per_device, scale),
        mesh=mesh,
        in_specs=(
            P("dp", "filter", "space", None),
            P(None, "filter", None),
            P("filter"),
            P("dp", "filter", "space", None),
        ),
        out_specs=(
            P("dp", "filter", "space", None),
            P("dp", "filter", "space", None),
            P(None, "filter", None),
            P("filter"),
        ),
        check_vma=False,
    )
```

time: 1240 us -> 67.9 us (0.05)
  waiting for transfers between devices: 768 us -> 0 us
  blocking collectives: 397 us -> 0 us
  Pallas kernels: 0 us -> 61.2 us
  local copies, waits for them, and re-layouts: 22.4 us -> 5.83 us
  between operations: 16.3 us -> 0.65 us
  other arithmetic: 14.7 us -> 0 us
    psum x1 -> x0, waiting for transfers between devices: 768 us -> none  [per_device(): weight_sum, bias_sum = lax.psum((weight_part, bias_part), ('dp', 'space'))]
    psum x1 -> x0, blocking collectives: 304 us -> none  [per_device(): weight_sum, bias_sum = lax.psum((weight_part, bias_part), ('dp', 'space'))]
    all_gather x2 -> x0, blocking collectives: 92.9 us -> none  [the longest x1 47.8 us: per_device(): padded = lax.all_gather(padded_local, 'filter', axis=1, tiled=True)[0]]
    pallas_call x0 -> x1, Pallas kernels: none -> 61.2 us  [per_device(): pl.pallas_call(functools.partial(kernel, scale), out_shape=[jax.ShapeDtyp...]
  transfers between devices with their start and end apart: 6 -> 0, of which waited for: 1 -> 0; matrix products, arithmetic and copies ran while one was open for 1% -> 0% of each run, Pallas kernels for 0% -> 0%
where the time goes in v1:
time: 67.9 us; the launch traced here: 67.6 us
  Pallas kernels  61.2 us (90%)
  local copies, waits for them, and re-layouts  5.83 us (9%)
    pallas_call x1, Pallas kernels, per_device(): pl.pallas_call(functools.partial(kernel, scale), out_shape=[jax.ShapeDtyp...  61.2 us
    unnamed x11, local copies, waits for them, and re-layouts  5.32 us

profile of v1, /device:TPU:1, one launch (start us, length us, event | category | flops | bytes accessed | tf_op | source)
XLA Modules:
  0.0 67.6 jit_solution(16979795282888838420)
XLA Ops:
  0.6 0.0 copy-start.3
  0.6 0.6 copy-done.3
  1.3 0.0 copy-start
  1.3 1.0 %copy-done = bf16[27,32,256]{2,1,0:T(8,128)(2,1)S(1)} copy-done((bf16[27,32,256]{2,1,0:T(8,128)(2,1)S(1)}, bf16[27,32,256]{2,1,0:T(8,128)(2,1)}, u32[]{:S(2)}) %copy-start) | copy-done | bytes 442392
  2.3 0.0 copy-start.1
  2.3 0.8 %copy-done.1 = bf16[1,32,1,512]{3,1,2,0:T(8,128)(2,1)S(1)} copy-done((bf16[1,32,1,512]{3,1,2,0:T(8,128)(2,1)S(1)}, bf16[1,32,1,512]{3,1,2,0:T(8,128)(2,1)}, u32[]{:S(2)}) %copy-start.1) | copy-done | bytes 32792
  3.1 0.0 copy-start.2
  3.1 0.8 %copy-done.2 = bf16[1,32,1,512]{3,1,2,0:T(8,128)(2,1)S(1)} copy-done((bf16[1,32,1,512]{3,1,2,0:T(8,128)(2,1)S(1)}, bf16[1,32,1,512]{3,1,2,0:T(8,128)(2,1)}, u32[]{:S(2)}) %copy-start.2) | copy-done | bytes 32792
  3.8 61.2 %shard_map.75 = (bf16[32,512]{1,0:T(8,128)(2,1)S(1)}, bf16[32,512]{1,0:T(8,128)(2,1)S(1)}, f32[27,32,256]{2,1,0:T(8,128)S(1)}, f32[1,128]{1,0:T(1,128)S(1)}) custom-call(bf16[32,512]{1,0:T(8,128)(2,1)S(1)} %bitcast.9, bf16[864,256]{1,0:T(8,128)(2,1)S(1)} %bitcast.8, f32[1,32]{1,0:T(1,128)S(1)} %bitcast.13, bf16[32,512]{1,0:T(8,128)(2,1)S(1)} %bitcast.10), custom_call_target="tpu_custom_call" | custom-call | tf_op jit(solution)/shard_map/pallas_call | solution.py:346
  65.0 0.5 slice_bitcast_fusion
  65.5 0.6 copy.11
  66.1 0.6 copy.12
  66.7 0.9 %copy.13 = f32[27,32,256]{2,1,0:T(8,128)} copy(f32[27,32,256]{2,1,0:T(8,128)S(1)} %get-tuple-element.18) | data formatting | bytes 1769472
Async XLA Ops:
  0.6 0.7 copy-start.3
  1.3 1.0 %copy-start = (bf16[27,32,256]{2,1,0:T(8,128)(2,1)S(1)}, bf16[27,32,256]{2,1,0:T(8,128)(2,1)}, u32[]{:S(2)}) copy-start(bf16[27,32,256]{2,1,0:T(8,128)(2,1)} %param.5) | copy-start | bytes 1327108
  2.3 0.8 %copy-start.1 = (bf16[1,32,1,512]{3,1,2,0:T(8,128)(2,1)S(1)}, bf16[1,32,1,512]{3,1,2,0:T(8,128)(2,1)}, u32[]{:S(2)}) copy-start(bf16[1,32,1,512]{3,1,2,0:T(8,128)(2,1)} %param.4) | copy-start | bytes 98308
  3.1 0.8 %copy-start.2 = (bf16[1,32,1,512]{3,1,2,0:T(8,128)(2,1)S(1)}, bf16[1,32,1,512]{3,1,2,0:T(8,128)(2,1)}, u32[]{:S(2)}) copy-start(bf16[1,32,1,512]{3,1,2,0:T(8,128)(2,1)} %param.7) | copy-start | bytes 98308

commit v2 on v1

--- a/solution.py
+++ b/solution.py
@@ -52,7 +52,7 @@
     vol, w, bias, cot,
     act_o, gin_o, gw_o, gb_o,
     V, COT, QS, QR, Q0, ACT, GN, GS, Fp, S, R0, T1, R1, O, N, RG,
-    z_send, z_recv, c_sem, q_send, q_recv, g_send, g_recv,
+    W, B, in_sem, z_send, z_recv, c_sem, q_send, q_recv, g_send, g_recv,
     d_sem, rs_send, rs_recv, ag_send, ag_recv, e_sem, n_send, n_recv,
 ):
     d = lax.axis_index("dp")
@@ -86,42 +86,49 @@
         pl.semaphore_signal(barrier, inc=1, device_id=at_z((z + k) % 16), device_id_type=MESH)
         pl.semaphore_signal(barrier, inc=1, device_id=at_xy((me + k) % 16), device_id_type=MESH)
     pl.semaphore_signal(barrier, inc=1, device_id=other, device_id_type=MESH)
+    loads = [
+        pltpu.make_async_copy(src, dst, in_sem.at[i])
+        for i, (src, dst) in enumerate(
+            ((vol, V.at[z]), (cot, COT.at[zh]), (w, W), (bias, B))
+        )
+    ]
+    for c in loads:
+        c.start()
+    loads[0].wait()
+    loads[1].wait()
     pl.semaphore_wait(barrier, 31)
 
-    even = z % 2 == 0
-    step2 = jnp.where(even, 2, -2)
-    nears = [near(1), near(-1), (z + step2 + 16) % 16]
-    fars = [near(4), near(-4), near(8)]
-    V[z] = vol[...]
-    COT[zh] = cot[...]
+    sign = 1 - 2 * (z % 2)
     sends = []
 
-    def shard(slot, to, i):
-        c = copy(V.at[slot], V.at[slot], z_send.at[i], z_recv.at[slot], at_z(to))
+    def shard(o, to):
+        slot = near(o)
+        c = copy(V.at[slot], V.at[slot], z_send.at[len(sends)], z_recv.at[slot], at_z(near(to)))
         c.start()
         sends.append(c)
 
-    def shard_wait(slot):
-        copy(V.at[slot], V.at[slot], z_send.at[0], z_recv.at[slot], at_z(nears[0])).wait_recv()
-
-    for i, to in enumerate(fars + nears):
-        shard(z, to, i)
-    for j, slot in enumerate(fars):
-        shard_wait(slot)
-        for i, to in enumerate(nears):
-            shard(slot, to, 6 + 3 * j + i)
+    def arrived(*offsets):
+        for o in offsets:
+            slot = near(o)
+            copy(V.at[slot], V.at[slot], z_send.at[0], z_recv.at[slot], at_z(near(1))).wait_recv()
+
     cot_copy = copy(COT.at[zh], COT.at[zh], c_sem.at[0], c_sem.at[1], at_z(near(8)))
+    for o in (5, -5, 2, -2, 1, -1):
+        shard(0, o)
+    arrived(5, -5)
+    shard(-5 * sign, 3 * sign)
+    for o in (5, -5):
+        for t in (2, -2, 1, -1):
+            shard(o, t)
     cot_copy.start()
-    sources = [near(1), near(-1), (z - step2 + 16) % 16]
-    for far in (0, 4, -4, 8):
-        for source in sources:
-            shard_wait((source + far + 16) % 16)
-
+    arrived(1, -1, 2, -2, 6, -4, -6, 4, 3, -3, 7, -7, 8)
+    loads[2].wait()
+    loads[3].wait()
     row_ok, col_ok = masks()
 
     def contribution(p, a):
         plane = V[8 * p : 8 * p + 8].reshape(CHANNELS, FACE)
-        taps = w[(a + 1) * 9 * ROWS : (a + 2) * 9 * ROWS, :]
+        taps = W[(a + 1) * 9 * ROWS : (a + 2) * 9 * ROWS, :]
         prod = jnp.dot(taps, plane, preferred_element_type=F32)
         total = None
         for c in (0, -1, 1):
@@ -162,7 +169,7 @@
     eye = lax.broadcasted_iota(jnp.int32, (ROWS, ROWS), 0) == lax.broadcasted_iota(
         jnp.int32, (ROWS, ROWS), 1
     )
-    column = jnp.sum(jnp.where(eye, bias[...], 0.0), axis=1, keepdims=True)
+    column = jnp.sum(jnp.where(eye, B[...], 0.0), axis=1, keepdims=True)
     first_plane = (y == 0) & (x == 0)
     last_plane = (y == 3) & (x == 3)
     cot_copy.wait_recv()
@@ -245,7 +252,7 @@
     d_copy.start()
 
     part = lax.dot_general(
-        w[...], GS[zh], (((0,), (0,)), ((), ())), preferred_element_type=F32
+        W[...], GS[zh], (((0,), (0,)), ((), ())), preferred_element_type=F32
     )
     for i in range(8):
         N[i] = part[i * ROWS : (i + 1) * ROWS].astype(BF16)
@@ -322,7 +329,7 @@
     finish(d)
     copy(O.at[1 - d], O.at[1 - d], e_sem.at[0], e_sem.at[1], other).wait_recv()
     finish(1 - d)
-    gb_o[...] = unpack(O[0, TAPS])[:, :128] * scale
+    gb_o[...] = unpack(O[0, TAPS])[:, :ROWS] * scale
 
     for c in sends + q_copies + g_copies + n_copies + [cot_copy, d_copy, e_copy]:
         c.wait_send()
@@ -340,18 +347,30 @@
             ).wait_send()
 
 
+def store(act, gin, gw, gb, act_o, gin_o, gw_o, gb_o, sem):
+    copies = [
+        pltpu.make_async_copy(src, dst, sem.at[i])
+        for i, (src, dst) in enumerate(((gw, gw_o), (act, act_o), (gin, gin_o), (gb, gb_o)))
+    ]
+    for c in copies:
+        c.start()
+    for c in copies:
+        c.wait()
+
+
 def per_device(scale, volumes, weight, bias, cotangent):
     vmem = pl.BlockSpec(memory_space=pltpu.VMEM)
+    hbm = pl.BlockSpec(memory_space=pltpu.HBM)
     dma = pltpu.SemaphoreType.DMA
     act, gin, gw, gb = pl.pallas_call(
         functools.partial(kernel, scale),
         out_shape=[
-            jax.ShapeDtypeStruct((ROWS, FACE), BF16),
-            jax.ShapeDtypeStruct((ROWS, FACE), BF16),
-            jax.ShapeDtypeStruct((TAPS, ROWS, CHANNELS), F32),
-            jax.ShapeDtypeStruct((1, 128), F32),
+            pltpu.VMEM((ROWS, FACE), BF16),
+            pltpu.VMEM((ROWS, FACE), BF16),
+            pltpu.VMEM((TAPS, ROWS, CHANNELS), F32),
+            pltpu.VMEM((1, ROWS), F32),
         ],
-        in_specs=[vmem] * 4,
+        in_specs=[hbm] * 4,
         out_specs=[vmem] * 4,
         scratch_shapes=[
             pltpu.VMEM((16, ROWS, FACE), BF16),
@@ -370,7 +389,9 @@
             pltpu.VMEM((2, UNITS, 16, CHANNELS), BF16),
             pltpu.VMEM((8, ROWS, FACE), BF16),
             pltpu.VMEM((8, ROWS, FACE), BF16),
-            dma((15,)), dma((16,)), dma((2,)),
+            pltpu.VMEM((TAPS * ROWS, CHANNELS), BF16),
+            pltpu.VMEM((1, ROWS), F32),
+            dma((4,)), dma((15,)), dma((16,)), dma((2,)),
             dma((2, 2)), dma((2, 2)), dma((2, 2)), dma((2, 2)),
             dma((2,)), dma((16,)), dma((16,)), dma((16,)), dma((16,)), dma((2,)),
             dma((8,)), dma((8,)),
@@ -379,13 +400,30 @@
             collective_id=0, has_side_effects=True, vmem_limit_bytes=48 * 2**20
         ),
     )(
-        volumes.reshape(ROWS, FACE),
-        weight.reshape(TAPS * ROWS, CHANNELS),
-        bias.reshape(1, ROWS),
-        cotangent.reshape(ROWS, FACE),
+        *(
+            pltpu.with_memory_space_constraint(a, pltpu.HBM)
+            for a in (
+                volumes.reshape(ROWS, FACE),
+                weight.reshape(TAPS * ROWS, CHANNELS),
+                bias.reshape(1, ROWS),
+                cotangent.reshape(ROWS, FACE),
+            )
+        )
     )
+    act, gin, gw, gb = pl.pallas_call(
+        store,
+        out_shape=[
+            jax.ShapeDtypeStruct((ROWS, FACE), BF16),
+            jax.ShapeDtypeStruct((ROWS, FACE), BF16),
+            jax.ShapeDtypeStruct((TAPS, ROWS, CHANNELS), F32),
+            jax.ShapeDtypeStruct((1, ROWS), F32),
+        ],
+        in_specs=[vmem] * 4,
+        out_specs=[hbm] * 4,
+        scratch_shapes=[dma((4,))],
+    )(*(pltpu.with_memory_space_constraint(a, pltpu.VMEM) for a in (act, gin, gw, gb)))
     shape = (1, ROWS, 1, FACE)
-    return act.reshape(shape), gin.reshape(shape), gw, gb[0, :ROWS]
+    return act.reshape(shape), gin.reshape(shape), gw, gb.reshape(ROWS)
 
 
 def solution(mesh):

time: 67.9 us -> 60.7 us (0.89)
  local copies, waits for them, and re-layouts: 5.83 us -> 0 us
  Pallas kernels: 61.2 us -> 59.9 us
    unnamed x11 -> x0, local copies, waits for them, and re-layouts: 5.32 us -> none
    pallas_call x1 -> x2, Pallas kernels: 61.2 us -> 59.9 us  [the longest x1 58.9 us: per_device(): pl.pallas_call(functools.partial(kernel, scale), out_shape=[pltpu.VMEM((R...]
where the time goes in v2:
time: 60.7 us; the launch traced here: 60.5 us
  Pallas kernels  59.9 us (99%)
  between operations  0.64 us (1%)
    pallas_call x1, Pallas kernels, per_device(): pl.pallas_call(functools.partial(kernel, scale), out_shape=[pltpu.VMEM((R...  58.9 us

profile of v2, /device:TPU:1, one launch (start us, length us, event | category | flops | bytes accessed | tf_op | source)
XLA Modules:
  0.0 60.5 jit_solution(6205008293629965820)
XLA Ops:
  0.6 58.9 %shard_map.75 = (bf16[32,512]{1,0:T(8,128)(2,1)S(1)}, bf16[32,512]{1,0:T(8,128)(2,1)S(1)}, f32[27,32,256]{2,1,0:T(8,128)S(1)}, f32[1,32]{1,0:T(1,128)S(1)}) custom-call(bf16[32,512]{1,0:T(8,128)(2,1)} %bitcast.8, bf16[864,256]{1,0:T(8,128)(2,1)} %bitcast.7, f32[1,32]{1,0:T(1,128)} %bitcast.10, bf16[32,512]{1,0:T(8,128)(2,1)} %bitcast.9), custom_call_target="tpu_custom_call" | custom-call | tf_op jit(solution)/shard_map/pallas_call | solution.py:365
  59.6 1.0 %shard_map.76 = (bf16[32,512]{1,0:T(8,128)(2,1)}, bf16[32,512]{1,0:T(8,128)(2,1)}, f32[27,32,256]{2,1,0:T(8,128)}, f32[1,32]{1,0:T(1,128)}) custom-call(bf16[32,512]{1,0:T(8,128)(2,1)S(1)} %get-tuple-element.12.act, bf16[32,512]{1,0:T(8,128)(2,1)S(1)} %get-tuple-element.13.gin, f32[27,32,256]{2,1,0:T(8,128)S(1)} %get-tuple-element.14.gw, ...), custom_call_target="tpu_custom_call" | custom-call | tf_op jit(solution)/shard_map/pallas_call | solution.py:413

commit v3 on v2

v3 whole, which is shorter than its diff:
```python
import functools
import math

import jax
import jax.numpy as jnp
from jax import lax
from jax.experimental import pallas as pl
from jax.experimental.pallas import tpu as pltpu
from jax.sharding import PartitionSpec as P

HEIGHT = 16
BREADTH = 32
FACE = HEIGHT * BREADTH
ROWS = 32
CHANNELS = 256
TAPS = 27
UNITS = 28
OWNERS = UNITS // 2
MESH = pl.DeviceIdType.MESH
F32 = jnp.float32
BF16 = jnp.bfloat16
SHIFTS = [(b, c) for b in (-1, 0, 1) for c in (-1, 0, 1)]


def masks():
    f = lax.broadcasted_iota(jnp.int32, (ROWS, FACE), 1)
    row, col = f // BREADTH, f % BREADTH
    row_ok = {b: (row + b >= 0) & (row + b < HEIGHT) for b in (-1, 1)}
    col_ok = {c: (col + c >= 0) & (col + c < BREADTH) for c in (-1, 1)}
    return row_ok, col_ok


def pull(x, amount, ok):
    return jnp.where(ok, pltpu.roll(x, (-amount) % FACE, 1), 0.0)


def pack(v):
    high = v.astype(BF16).astype(F32)
    low = v - high
    row = lax.broadcasted_iota(jnp.int32, (16, CHANNELS), 0)
    return jnp.where(row == 0, high, jnp.where(row == 1, low, 0.0)).astype(BF16)


def unpack(unit):
    u = unit.astype(F32)
    row = lax.broadcasted_iota(jnp.int32, u.shape, 0)
    return jnp.sum(jnp.where(row < 2, u, 0.0), axis=0, keepdims=True)


def kernel(
    scale,
    vol, w, bias, cot,
    act_o, gin_o, gw_o, gb_o,
    V, COT, ACT, GN, GS, Fp, S, R0, T1, R1, O, N, RG, W, WT, B,
    in_sem, z_send, z_recv, x_send, x_recv, c_sem, g_send, g_recv,
    d_sem, rs_send, rs_recv, ag_send, ag_recv, e_sem, n_send, n_recv,
):
    d = lax.axis_index("dp")
    s = lax.axis_index("space")
    f = lax.axis_index("filter")
    y = s // 8
    zh = (s // 4) % 2
    x = s % 4
    z = zh * 8 + f
    me = y * 4 + x
    sign = 1 - 2 * (z % 2)

    def at_z(k):
        return (d, y * 8 + (k // 8) * 4 + x, k % 8)

    def at_xy(j):
        return (d, (j // 4) * 8 + zh * 4 + j % 4, f)

    def near(k):
        return (z + k + 16) % 16

    other = (1 - d, s, f)

    def copy(src, dst, send, recv, to):
        return pltpu.make_async_remote_copy(
            src_ref=src, dst_ref=dst, send_sem=send, recv_sem=recv,
            device_id=to, device_id_type=MESH,
        )

    barrier = pltpu.get_barrier_semaphore()
    for k in range(1, 16):
        pl.semaphore_signal(barrier, inc=1, device_id=at_z((z + k) % 16), device_id_type=MESH)
        pl.semaphore_signal(barrier, inc=1, device_id=at_xy((me + k) % 16), device_id_type=MESH)
    pl.semaphore_signal(barrier, inc=1, device_id=other, device_id_type=MESH)
    loads = [
        pltpu.make_async_copy(src, dst, in_sem.at[i])
        for i, (src, dst) in enumerate(
            ((vol, V.at[zh, 1, f]), (cot, COT.at[zh]), (w, W), (bias, B))
        )
    ]
    for c in loads:
        c.start()
    loads[0].wait()
    loads[1].wait()
    pl.semaphore_wait(barrier, 31)

    def after(p):
        last = x == 3
        x2 = (x + 1) % 4
        y2 = (y + jnp.where(last, p, 0)) % 4
        return y2 * 4 + x2, jnp.where(last, 1 - p, p)

    def before(p):
        first = x == 0
        x2 = (x + 3) % 4
        y2 = (y + 4 - jnp.where(first, 1 - p, 0)) % 4
        return y2 * 4 + x2, jnp.where(first, 1 - p, p)

    sends = []
    x_copies = []

    def place(slot):
        return V.at[slot // 8, 1, slot % 8]

    def shard(o, to):
        slot = near(o)
        c = copy(place(slot), place(slot), z_send.at[len(sends)], z_recv.at[slot], at_z(near(to)))
        c.start()
        sends.append(c)

    def beside(*offsets):
        for o in offsets:
            slot = near(o)
            p, i = slot // 8, slot % 8
            for side, where in ((0, after), (2, before)):
                j, q = where(p)
                c = copy(
                    place(slot), V.at[q, side, i],
                    x_send.at[len(x_copies)], x_recv.at[q, side // 2, i], at_xy(j),
                )
                c.start()
                x_copies.append(c)

    def arrived(*offsets):
        for o in offsets:
            slot = near(o)
            copy(place(slot), place(slot), z_send.at[0], z_recv.at[slot], at_z(near(1))).wait_recv()

    cot_copy = copy(COT.at[zh], COT.at[zh], c_sem.at[0], c_sem.at[1], at_z(near(8)))
    for o in (3, -3, 1, -1):
        shard(0, o)
    beside(0)
    loads[2].wait()
    loads[3].wait()
    WT[...] = W[...].T
    for o in (1, -1):
        arrived(o)
        beside(o)
    for o in (3, -3):
        arrived(o)
        for t in (-o, 1, -1):
            shard(o, t)
    beside(3, -3)

    for o in (2, -2):
        arrived(o)
        beside(o)
    for o in (6, -6):
        arrived(o)
        for t in (1, -1):
            shard(o, t)
    for o in (4, -4):
        arrived(o)
        beside(o)
    beside(6, -6)
    cot_copy.start()
    for o in (5, -5):
        arrived(o)
        beside(o)
    arrived(-7 * sign)
    shard(-7 * sign, sign)
    beside(-7 * sign)
    for o in (7 * sign, 8):
        arrived(o)
        beside(o)
    for p in (0, 1):
        for side in (0, 2):
            for i in range(8):
                copy(
                    V.at[p, side, i], V.at[p, side, i],
                    x_send.at[0], x_recv.at[p, side // 2, i], at_xy((me + 1) % 16),
                ).wait_recv()

    first_plane = (y == 0) & (x == 0)
    last_plane = (y == 3) & (x == 3)

    @pl.when(first_plane)
    def _():
        V[0, 0] = jnp.zeros((8, ROWS, FACE), BF16)

    @pl.when(last_plane)
    def _():
        V[1, 2] = jnp.zeros((8, ROWS, FACE), BF16)

    row_ok, col_ok = masks()
    eye = lax.broadcasted_iota(jnp.int32, (ROWS, ROWS), 0) == lax.broadcasted_iota(
        jnp.int32, (ROWS, ROWS), 1
    )
    column = jnp.sum(jnp.where(eye, B[...], 0.0), axis=1, keepdims=True)

    def pre_activation(p):
        taps = jnp.concatenate([W[a * 9 * ROWS : (a + 1) * 9 * ROWS] for a in range(3)], axis=1)
        planes = V[p].reshape(3 * CHANNELS, FACE)
        prod = jnp.dot(taps, planes, preferred_element_type=F32)
        total = column
        for c in (0, -1, 1):
            part = None
            for b in (0, -1, 1):
                i = 3 * (b + 1) + (c + 1)
                term = prod[i * ROWS : (i + 1) * ROWS]
                if b:
                    term = pull(term, BREADTH * b, row_ok[b])
                part = term if part is None else part + term
            if c:
                part = pull(part, c, col_ok[c])
            total = total + part
        return total

    def shifted(p, a, grad):
        for c in (-1, 0, 1):
            moved = pull(grad, -c, col_ok[-c]) if c else grad
            for b in (-1, 0, 1):
                i = 3 * (b + 1) + (c + 1)
                term = pull(moved, -BREADTH * b, row_ok[-b]) if b else moved
                GS[p, a + 1, i * ROWS : (i + 1) * ROWS, :] = term.astype(BF16)

    cot_copy.wait_recv()
    g_copies = []
    bias_total = jnp.zeros((ROWS, 1), F32)
    for p in (0, 1):
        pre = pre_activation(p)
        sig = jax.nn.sigmoid(pre)
        grad = (COT[p].astype(F32) * sig * (1.0 + pre * (1.0 - sig))).astype(BF16)
        GN[p, 1] = grad
        for side, slot, where in ((0, 2, after), (1, 0, before)):
            j, q = where(p)
            c = copy(GN.at[p, 1], GN.at[q, slot], g_send.at[p, side], g_recv.at[q, side], at_xy(j))
            c.start()
            g_copies.append(c)
        ACT[p] = (pre * sig).astype(BF16)
        grad = grad.astype(F32)
        bias_total = bias_total + jnp.sum(grad, axis=1, keepdims=True)
        shifted(p, 0, grad)

    total = None
    for p in (0, 1):
        term = lax.dot_general(
            GS[p, 1], V[p].reshape(3 * CHANNELS, FACE),
            (((1,), (1,)), ((), ())), preferred_element_type=F32,
        )
        total = term if total is None else total + term
    for a in range(3):
        for i in range(9):
            for h in (0, 1):
                piece = total[
                    i * ROWS + h * 16 : i * ROWS + (h + 1) * 16,
                    a * CHANNELS : (a + 1) * CHANNELS,
                ]
                Fp[h, 9 * a + i] = piece
                S[h, 9 * a + i] = piece.astype(BF16)
    eye = lax.broadcasted_iota(jnp.int32, (ROWS, CHANNELS), 0) == lax.broadcasted_iota(
        jnp.int32, (ROWS, CHANNELS), 1
    )
    bias_row = jnp.sum(jnp.where(eye, bias_total, 0.0), axis=0, keepdims=True)
    for h in (0, 1):
        Fp[h, TAPS] = jnp.broadcast_to(bias_row, (16, CHANNELS))
        S[h, TAPS] = pack(bias_row)

    d_copy = copy(S.at[1 - d], R0, d_sem.at[0], d_sem.at[1], other)
    d_copy.start()
    act_o[...] = ACT[zh]
    d_copy.wait_recv()
    summed = Fp[d] + R0[...].astype(F32)
    T1[...] = summed.astype(BF16)
    T1[TAPS] = pack(Fp[d, TAPS, 0:1, :] + unpack(R0[TAPS]))

    def mine(ref, j):
        return ref.at[pl.ds(2 * j, 2)]

    def rs_copy(k):
        to = (me + k) % 16
        return to, copy(mine(T1, to), mine(R1, me), rs_send.at[k], rs_recv.at[me], at_xy(to))

    for k in range(1, 16):
        to, c = rs_copy(k)
        pl.when(to < OWNERS)(c.start)

    for p in (0, 1):
        for side, slot in ((0, 2), (1, 0)):
            copy(
                GN.at[p, 1], GN.at[p, slot], g_send.at[p, side], g_recv.at[p, side], other
            ).wait_recv()
    for p in (0, 1):
        for a in (-1, 1):
            grad = GN[p, a + 1].astype(F32)
            if p == 0 and a == 1:
                grad = jnp.where(first_plane, 0.0, grad)
            if p == 1 and a == -1:
                grad = jnp.where(last_plane, 0.0, grad)
            shifted(p, a, grad)
        part = jnp.dot(
            WT[...], GS[p].reshape(TAPS * ROWS, FACE), preferred_element_type=F32
        )
        for i in range(8):
            N[p, i] = part[i * ROWS : (i + 1) * ROWS].astype(BF16)
    n_copies = []
    for i, o in enumerate((-4 * sign, 3, -3, 2, -2, 1, -1)):
        to = near(o)
        c = copy(N.at[to // 8, to % 8], RG.at[i], n_send.at[i], n_recv.at[i], at_z(to))
        c.start()
        n_copies.append(c)

    @pl.when(me < OWNERS)
    def _():
        R1[pl.ds(2 * me, 2)] = T1[pl.ds(2 * me, 2)]
        for k in range(1, 16):
            source = (me + k) % 16
            copy(
                mine(T1, me), mine(R1, source), rs_send.at[k], rs_recv.at[source], at_xy(source)
            ).wait_recv()
        total = R1[0:2].astype(F32)
        for i in range(1, 16):
            total = total + R1[2 * i : 2 * i + 2].astype(F32)
        O[d, pl.ds(2 * me, 2)] = total.astype(BF16)

        @pl.when(me == OWNERS - 1)
        def _():
            O[d, TAPS] = pack(jnp.sum(total[1, 0:2], axis=0, keepdims=True))

        for k in range(1, 16):
            to = (me + k) % 16
            copy(
                O.at[d, pl.ds(2 * me, 2)], O.at[d, pl.ds(2 * me, 2)],
                ag_send.at[k], ag_recv.at[me], at_xy(to),
            ).start()

    for k in range(1, 16):
        source = (me + k) % 16

        @pl.when(source < OWNERS)
        def _():
            copy(
                O.at[d, pl.ds(2 * source, 2)], O.at[d, pl.ds(2 * source, 2)],
                ag_send.at[k], ag_recv.at[source], at_xy(source),
            ).wait_recv()

    e_copy = copy(O.at[d], O.at[d], e_sem.at[0], e_sem.at[1], other)
    e_copy.start()

    def finish(h):
        gw_o[:, pl.ds(pl.multiple_of(h * 16, 16), 16), :] = O[h, 0:TAPS].astype(F32) * scale

    finish(d)
    own = N[zh, f].astype(F32)
    for c in n_copies:
        c.wait_recv()
    for i in range(7):
        own = own + RG[i].astype(F32)
    gin_o[...] = own.astype(BF16)
    copy(O.at[1 - d], O.at[1 - d], e_sem.at[0], e_sem.at[1], other).wait_recv()
    finish(1 - d)
    gb_o[...] = unpack(O[0, TAPS])[:, :ROWS] * scale

    for c in sends + x_copies + g_copies + n_copies + [cot_copy, d_copy, e_copy]:
        c.wait_send()
    for k in range(1, 16):
        to, c = rs_copy(k)
        pl.when(to < OWNERS)(c.wait_send)

    @pl.when(me < OWNERS)
    def _():
        for k in range(1, 16):
            to = (me + k) % 16
            copy(
                O.at[d, pl.ds(2 * me, 2)], O.at[d, pl.ds(2 * me, 2)],
                ag_send.at[k], ag_recv.at[me], at_xy(to),
            ).wait_send()


def store(act, gin, gw, gb, act_o, gin_o, gw_o, gb_o, sem):
    copies = [
        pltpu.make_async_copy(src, dst, sem.at[i])
        for i, (src, dst) in enumerate(((gw, gw_o), (act, act_o), (gin, gin_o), (gb, gb_o)))
    ]
    for c in copies:
        c.start()
    for c in copies:
        c.wait()


def per_device(scale, volumes, weight, bias, cotangent):
    vmem = pl.BlockSpec(memory_space=pltpu.VMEM)
    hbm = pl.BlockSpec(memory_space=pltpu.HBM)
    dma = pltpu.SemaphoreType.DMA
    act, gin, gw, gb = pl.pallas_call(
        functools.partial(kernel, scale),
        out_shape=[
            pltpu.VMEM((ROWS, FACE), BF16),
            pltpu.VMEM((ROWS, FACE), BF16),
            pltpu.VMEM((TAPS, ROWS, CHANNELS), F32),
            pltpu.VMEM((1, ROWS), F32),
        ],
        in_specs=[hbm] * 4,
        out_specs=[vmem] * 4,
        scratch_shapes=[
            pltpu.VMEM((2, 3, 8, ROWS, FACE), BF16),
            pltpu.VMEM((2, ROWS, FACE), BF16),
            pltpu.VMEM((2, ROWS, FACE), BF16),
            pltpu.VMEM((2, 3, ROWS, FACE), BF16),
            pltpu.VMEM((2, 3, 9 * ROWS, FACE), BF16),
            pltpu.VMEM((2, UNITS, 16, CHANNELS), F32),
            pltpu.VMEM((2, UNITS, 16, CHANNELS), BF16),
            pltpu.VMEM((UNITS, 16, CHANNELS), BF16),
            pltpu.VMEM((UNITS, 16, CHANNELS), BF16),
            pltpu.VMEM((32, 16, CHANNELS), BF16),
            pltpu.VMEM((2, UNITS, 16, CHANNELS), BF16),
            pltpu.VMEM((2, 8, ROWS, FACE), BF16),
            pltpu.VMEM((7, ROWS, FACE), BF16),
            pltpu.VMEM((TAPS * ROWS, CHANNELS), BF16),
            pltpu.VMEM((CHANNELS, TAPS * ROWS), BF16),
            pltpu.VMEM((1, ROWS), F32),
            dma((4,)), dma((15,)), dma((16,)), dma((32,)), dma((2, 2, 8)), dma((2,)),
            dma((2, 2)), dma((2, 2)),
            dma((2,)), dma((16,)), dma((16,)), dma((16,)), dma((16,)), dma((2,)),
            dma((7,)), dma((7,)),
        ],
        compiler_params=pltpu.CompilerParams(
            collective_id=0, has_side_effects=True, vmem_limit_bytes=48 * 2**20
        ),
    )(
        *(
            pltpu.with_memory_space_constraint(a, pltpu.HBM)
            for a in (
                volumes.reshape(ROWS, FACE),
                weight.reshape(TAPS * ROWS, CHANNELS),
                bias.reshape(1, ROWS),
                cotangent.reshape(ROWS, FACE),
            )
        )
    )
    act, gin, gw, gb = pl.pallas_call(
        store,
        out_shape=[
            jax.ShapeDtypeStruct((ROWS, FACE), BF16),
            jax.ShapeDtypeStruct((ROWS, FACE), BF16),
            jax.ShapeDtypeStruct((TAPS, ROWS, CHANNELS), F32),
            jax.ShapeDtypeStruct((1, ROWS), F32),
        ],
        in_specs=[vmem] * 4,
        out_specs=[hbm] * 4,
        scratch_shapes=[dma((4,))],
    )(*(pltpu.with_memory_space_constraint(a, pltpu.VMEM) for a in (act, gin, gw, gb)))
    shape = (1, ROWS, 1, FACE)
    return act.reshape(shape), gin.reshape(shape), gw, gb.reshape(ROWS)


def solution(mesh):
    scale = 1.0 / math.sqrt(2 * 32 * FACE)
    return jax.shard_map(
        functools.partial(per_device, scale),
        mesh=mesh,
        in_specs=(
            P("dp", "filter", "space", None),
            P(None, "filter", None),
            P("filter"),
            P("dp", "filter", "space", None),
        ),
        out_specs=(
            P("dp", "filter", "space", None),
            P("dp", "filter", "space", None),
            P(None, "filter", None),
            P("filter"),
        ),
        check_vma=False,
    )
```

time: 60.7 us -> 58.1 us (0.957)
  Pallas kernels: 59.9 us -> 57.4 us
    pallas_call x1, Pallas kernels: 58.9 us -> 56.4 us  [per_device(): pl.pallas_call(functools.partial(kernel, scale), out_shape=[pltpu.VMEM((R...]
where the time goes in v3:
time: 58.1 us; the launch traced here: 58 us
  Pallas kernels  57.4 us (99%)
  between operations  0.64 us (1%)
    pallas_call x1, Pallas kernels, per_device(): pl.pallas_call(functools.partial(kernel, scale), out_shape=[pltpu.VMEM((R...  56.4 us

profile of v3, /device:TPU:1, one launch (start us, length us, event | category | flops | bytes accessed | tf_op | source)
XLA Modules:
  0.0 58.0 jit_solution(4877283014094647799)
XLA Ops:
  0.6 56.4 %shard_map.75 = (bf16[32,512]{1,0:T(8,128)(2,1)S(1)}, bf16[32,512]{1,0:T(8,128)(2,1)S(1)}, f32[27,32,256]{2,1,0:T(8,128)S(1)}, f32[1,32]{1,0:T(1,128)S(1)}) custom-call(bf16[32,512]{1,0:T(8,128)(2,1)} %bitcast.8, bf16[864,256]{1,0:T(8,128)(2,1)} %bitcast.7, f32[1,32]{1,0:T(1,128)} %bitcast.10, bf16[32,512]{1,0:T(8,128)(2,1)} %bitcast.9), custom_call_target="tpu_custom_call" | custom-call | tf_op jit(solution)/shard_map/pallas_call | solution.py:400
  57.1 1.0 %shard_map.76 = (bf16[32,512]{1,0:T(8,128)(2,1)}, bf16[32,512]{1,0:T(8,128)(2,1)}, f32[27,32,256]{2,1,0:T(8,128)}, f32[1,32]{1,0:T(1,128)}) custom-call(bf16[32,512]{1,0:T(8,128)(2,1)S(1)} %get-tuple-element.12.act, bf16[32,512]{1,0:T(8,128)(2,1)S(1)} %get-tuple-element.13.gin, f32[27,32,256]{2,1,0:T(8,128)S(1)} %get-tuple-element.14.gw, ...), custom_call_target="tpu_custom_call" | custom-call | tf_op jit(solution)/shard_map/pallas_call | solution.py:446

commit v4 on v3

--- a/solution.py
+++ b/solution.py
@@ -156,26 +156,17 @@
         for t in (-o, 1, -1):
             shard(o, t)
     beside(3, -3)
-
-    for o in (2, -2):
+    for o in (2, -2, 4, -4):
         arrived(o)
         beside(o)
     for o in (6, -6):
         arrived(o)
         for t in (1, -1):
             shard(o, t)
-    for o in (4, -4):
-        arrived(o)
-        beside(o)
+    shard(-6 * sign, 2 * sign)
     beside(6, -6)
     cot_copy.start()
-    for o in (5, -5):
-        arrived(o)
-        beside(o)
-    arrived(-7 * sign)
-    shard(-7 * sign, sign)
-    beside(-7 * sign)
-    for o in (7 * sign, 8):
+    for o in (5, -5, 7, -7, 8):
         arrived(o)
         beside(o)
     for p in (0, 1):

time: 58.1 us -> 56.4 us (0.971)
  Pallas kernels: 57.4 us -> 55.6 us
    pallas_call x1, Pallas kernels: 56.4 us -> 54.6 us  [per_device(): pl.pallas_call(functools.partial(kernel, scale), out_shape=[pltpu.VMEM((R...]
where the time goes in v4:
time: 56.4 us; the launch traced here: 56.2 us
  Pallas kernels  55.6 us (99%)
  between operations  0.64 us (1%)
    pallas_call x1, Pallas kernels, per_device(): pl.pallas_call(functools.partial(kernel, scale), out_shape=[pltpu.VMEM((R...  54.6 us

profile of v4, /device:TPU:1, one launch (start us, length us, event | category | flops | bytes accessed | tf_op | source)
XLA Modules:
  0.0 56.2 jit_solution(15570600572981780313)
XLA Ops:
  0.6 54.6 %shard_map.75 = (bf16[32,512]{1,0:T(8,128)(2,1)S(1)}, bf16[32,512]{1,0:T(8,128)(2,1)S(1)}, f32[27,32,256]{2,1,0:T(8,128)S(1)}, f32[1,32]{1,0:T(1,128)S(1)}) custom-call(bf16[32,512]{1,0:T(8,128)(2,1)} %bitcast.8, bf16[864,256]{1,0:T(8,128)(2,1)} %bitcast.7, f32[1,32]{1,0:T(1,128)} %bitcast.10, bf16[32,512]{1,0:T(8,128)(2,1)} %bitcast.9), custom_call_target="tpu_custom_call" | custom-call | tf_op jit(solution)/shard_map/pallas_call | solution.py:391
  55.3 1.0 %shard_map.76 = (bf16[32,512]{1,0:T(8,128)(2,1)}, bf16[32,512]{1,0:T(8,128)(2,1)}, f32[27,32,256]{2,1,0:T(8,128)}, f32[1,32]{1,0:T(1,128)}) custom-call(bf16[32,512]{1,0:T(8,128)(2,1)S(1)} %get-tuple-element.12.act, bf16[32,512]{1,0:T(8,128)(2,1)S(1)} %get-tuple-element.13.gin, f32[27,32,256]{2,1,0:T(8,128)S(1)} %get-tuple-element.14.gw, ...), custom_call_target="tpu_custom_call" | custom-call | tf_op jit(solution)/shard_map/pallas_call | solution.py:437

commit v5 on v4

--- a/solution.py
+++ b/solution.py
@@ -16,6 +16,7 @@
 TAPS = 27
 UNITS = 28
 OWNERS = UNITS // 2
+FAR = sorted(range(1, 16), key=lambda k: -min(k // 4, 4 - k // 4) - min(k % 4, 4 - k % 4))
 MESH = pl.DeviceIdType.MESH
 F32 = jnp.float32
 BF16 = jnp.bfloat16
@@ -51,7 +52,7 @@
     scale,
     vol, w, bias, cot,
     act_o, gin_o, gw_o, gb_o,
-    V, COT, ACT, GN, GS, Fp, S, R0, T1, R1, O, N, RG, W, WT, B,
+    V, COT, CR, ACT, GN, GS, Fp, S, R0, T1, R1, O, N, RG, W, WT, B,
     in_sem, z_send, z_recv, x_send, x_recv, c_sem, g_send, g_recv,
     d_sem, rs_send, rs_recv, ag_send, ag_recv, e_sem, n_send, n_recv,
 ):
@@ -83,8 +84,9 @@
         )
 
     barrier = pltpu.get_barrier_semaphore()
+    for k in (1, -1, 2, -2, 3, -3, 4, -4):
+        pl.semaphore_signal(barrier, inc=1, device_id=at_z(near(k)), device_id_type=MESH)
     for k in range(1, 16):
-        pl.semaphore_signal(barrier, inc=1, device_id=at_z((z + k) % 16), device_id_type=MESH)
         pl.semaphore_signal(barrier, inc=1, device_id=at_xy((me + k) % 16), device_id_type=MESH)
     pl.semaphore_signal(barrier, inc=1, device_id=other, device_id_type=MESH)
     loads = [
@@ -97,7 +99,7 @@
         c.start()
     loads[0].wait()
     loads[1].wait()
-    pl.semaphore_wait(barrier, 31)
+    pl.semaphore_wait(barrier, 24)
 
     def after(p):
         last = x == 3
@@ -141,7 +143,9 @@
             slot = near(o)
             copy(place(slot), place(slot), z_send.at[0], z_recv.at[slot], at_z(near(1))).wait_recv()
 
-    cot_copy = copy(COT.at[zh], COT.at[zh], c_sem.at[0], c_sem.at[1], at_z(near(8)))
+    half = near(-4 * sign) // 8
+    cot_first = copy(COT.at[zh], CR, c_sem.at[0], c_sem.at[1], at_z(near(4 * sign)))
+    cot_copy = copy(CR, COT.at[half], c_sem.at[2], c_sem.at[3], at_z(near(4 * sign)))
     for o in (3, -3, 1, -1):
         shard(0, o)
     beside(0)
@@ -155,6 +159,7 @@
         arrived(o)
         for t in (-o, 1, -1):
             shard(o, t)
+    cot_first.start()
     beside(3, -3)
     for o in (2, -2, 4, -4):
         arrived(o)
@@ -165,6 +170,7 @@
             shard(o, t)
     shard(-6 * sign, 2 * sign)
     beside(6, -6)
+    cot_first.wait_recv()
     cot_copy.start()
     for o in (5, -5, 7, -7, 8):
         arrived(o)
@@ -273,11 +279,14 @@
     def mine(ref, j):
         return ref.at[pl.ds(2 * j, 2)]
 
+    def beyond(k):
+        return ((y + k // 4) % 4) * 4 + (x + k) % 4
+
     def rs_copy(k):
-        to = (me + k) % 16
+        to = beyond(k)
         return to, copy(mine(T1, to), mine(R1, me), rs_send.at[k], rs_recv.at[me], at_xy(to))
 
-    for k in range(1, 16):
+    for k in FAR:
         to, c = rs_copy(k)
         pl.when(to < OWNERS)(c.start)
 
@@ -323,8 +332,8 @@
         def _():
             O[d, TAPS] = pack(jnp.sum(total[1, 0:2], axis=0, keepdims=True))
 
-        for k in range(1, 16):
-            to = (me + k) % 16
+        for k in FAR:
+            to = beyond(k)
             copy(
                 O.at[d, pl.ds(2 * me, 2)], O.at[d, pl.ds(2 * me, 2)],
                 ag_send.at[k], ag_recv.at[me], at_xy(to),
@@ -357,7 +366,7 @@
     finish(1 - d)
     gb_o[...] = unpack(O[0, TAPS])[:, :ROWS] * scale
 
-    for c in sends + x_copies + g_copies + n_copies + [cot_copy, d_copy, e_copy]:
+    for c in sends + x_copies + g_copies + n_copies + [cot_first, cot_copy, d_copy, e_copy]:
         c.wait_send()
     for k in range(1, 16):
         to, c = rs_copy(k)
@@ -401,6 +410,7 @@
         scratch_shapes=[
             pltpu.VMEM((2, 3, 8, ROWS, FACE), BF16),
             pltpu.VMEM((2, ROWS, FACE), BF16),
+            pltpu.VMEM((ROWS, FACE), BF16),
             pltpu.VMEM((2, ROWS, FACE), BF16),
             pltpu.VMEM((2, 3, ROWS, FACE), BF16),
             pltpu.VMEM((2, 3, 9 * ROWS, FACE), BF16),
@@ -415,7 +425,7 @@
             pltpu.VMEM((TAPS * ROWS, CHANNELS), BF16),
             pltpu.VMEM((CHANNELS, TAPS * ROWS), BF16),
             pltpu.VMEM((1, ROWS), F32),
-            dma((4,)), dma((15,)), dma((16,)), dma((32,)), dma((2, 2, 8)), dma((2,)),
+            dma((4,)), dma((15,)), dma((16,)), dma((32,)), dma((2, 2, 8)), dma((4,)),
             dma((2, 2)), dma((2, 2)),
             dma((2,)), dma((16,)), dma((16,)), dma((16,)), dma((16,)), dma((2,)),
             dma((7,)), dma((7,)),

time: 56.4 us -> 54.4 us (0.965)
  Pallas kernels: 55.6 us -> 53.6 us
    pallas_call x1, Pallas kernels: 54.6 us -> 52.7 us  [per_device(): pl.pallas_call(functools.partial(kernel, scale), out_shape=[pltpu.VMEM((R...]
where the time goes in v5:
time: 54.4 us; the launch traced here: 54.3 us
  Pallas kernels  53.6 us (99%)
  between operations  0.64 us (1%)
    pallas_call x1, Pallas kernels, per_device(): pl.pallas_call(functools.partial(kernel, scale), out_shape=[pltpu.VMEM((R...  52.7 us

profile of v5, /device:TPU:1, one launch (start us, length us, event | category | flops | bytes accessed | tf_op | source)
XLA Modules:
  0.0 54.3 jit_solution(8728557810384901690)
XLA Ops:
  0.6 52.7 %shard_map.75 = (bf16[32,512]{1,0:T(8,128)(2,1)S(1)}, bf16[32,512]{1,0:T(8,128)(2,1)S(1)}, f32[27,32,256]{2,1,0:T(8,128)S(1)}, f32[1,32]{1,0:T(1,128)S(1)}) custom-call(bf16[32,512]{1,0:T(8,128)(2,1)} %bitcast.8, bf16[864,256]{1,0:T(8,128)(2,1)} %bitcast.7, f32[1,32]{1,0:T(1,128)} %bitcast.10, bf16[32,512]{1,0:T(8,128)(2,1)} %bitcast.9), custom_call_target="tpu_custom_call" | custom-call | tf_op jit(solution)/shard_map/pallas_call | solution.py:400
  53.3 1.0 %shard_map.76 = (bf16[32,512]{1,0:T(8,128)(2,1)}, bf16[32,512]{1,0:T(8,128)(2,1)}, f32[27,32,256]{2,1,0:T(8,128)}, f32[1,32]{1,0:T(1,128)}) custom-call(bf16[32,512]{1,0:T(8,128)(2,1)S(1)} %get-tuple-element.12.act, bf16[32,512]{1,0:T(8,128)(2,1)S(1)} %get-tuple-element.13.gin, f32[27,32,256]{2,1,0:T(8,128)S(1)} %get-tuple-element.14.gw, ...), custom_call_target="tpu_custom_call" | custom-call | tf_op jit(solution)/shard_map/pallas_call | solution.py:447

commit v6 on v5

--- a/solution.py
+++ b/solution.py
@@ -271,25 +271,6 @@
     d_copy = copy(S.at[1 - d], R0, d_sem.at[0], d_sem.at[1], other)
     d_copy.start()
     act_o[...] = ACT[zh]
-    d_copy.wait_recv()
-    summed = Fp[d] + R0[...].astype(F32)
-    T1[...] = summed.astype(BF16)
-    T1[TAPS] = pack(Fp[d, TAPS, 0:1, :] + unpack(R0[TAPS]))
-
-    def mine(ref, j):
-        return ref.at[pl.ds(2 * j, 2)]
-
-    def beyond(k):
-        return ((y + k // 4) % 4) * 4 + (x + k) % 4
-
-    def rs_copy(k):
-        to = beyond(k)
-        return to, copy(mine(T1, to), mine(R1, me), rs_send.at[k], rs_recv.at[me], at_xy(to))
-
-    for k in FAR:
-        to, c = rs_copy(k)
-        pl.when(to < OWNERS)(c.start)
-
     for p in (0, 1):
         for side, slot in ((0, 2), (1, 0)):
             copy(
@@ -303,6 +284,26 @@
             if p == 1 and a == -1:
                 grad = jnp.where(last_plane, 0.0, grad)
             shifted(p, a, grad)
+    d_copy.wait_recv()
+    summed = Fp[d] + R0[...].astype(F32)
+    T1[...] = summed.astype(BF16)
+    T1[TAPS] = pack(Fp[d, TAPS, 0:1, :] + unpack(R0[TAPS]))
+
+    def mine(ref, j):
+        return ref.at[pl.ds(2 * j, 2)]
+
+    def beyond(k):
+        return ((y + k // 4) % 4) * 4 + (x + k) % 4
+
+    def rs_copy(k):
+        to = beyond(k)
+        return to, copy(mine(T1, to), mine(R1, me), rs_send.at[k], rs_recv.at[me], at_xy(to))
+
+    for k in FAR:
+        to, c = rs_copy(k)
+        pl.when(to < OWNERS)(c.start)
+
+    for p in (0, 1):
         part = jnp.dot(
             WT[...], GS[p].reshape(TAPS * ROWS, FACE), preferred_element_type=F32
         )

time: 54.4 us -> 57.1 us (1.050)
  Pallas kernels: 53.6 us -> 56.3 us
    pallas_call x1, Pallas kernels: 52.7 us -> 55.4 us  [per_device(): pl.pallas_call(functools.partial(kernel, scale), out_shape=[pltpu.VMEM((R...]
where the time goes in v6:
time: 57.1 us; the launch traced here: 57 us
  Pallas kernels  56.3 us (99%)
  between operations  0.64 us (1%)
    pallas_call x1, Pallas kernels, per_device(): pl.pallas_call(functools.partial(kernel, scale), out_shape=[pltpu.VMEM((R...  55.4 us

profile of v6, /device:TPU:1, one launch (start us, length us, event | category | flops | bytes accessed | tf_op | source)
XLA Modules:
  0.0 57.0 jit_solution(5875139686072613507)
XLA Ops:
  0.6 55.4 %shard_map.75 = (bf16[32,512]{1,0:T(8,128)(2,1)S(1)}, bf16[32,512]{1,0:T(8,128)(2,1)S(1)}, f32[27,32,256]{2,1,0:T(8,128)S(1)}, f32[1,32]{1,0:T(1,128)S(1)}) custom-call(bf16[32,512]{1,0:T(8,128)(2,1)} %bitcast.8, bf16[864,256]{1,0:T(8,128)(2,1)} %bitcast.7, f32[1,32]{1,0:T(1,128)} %bitcast.10, bf16[32,512]{1,0:T(8,128)(2,1)} %bitcast.9), custom_call_target="tpu_custom_call" | custom-call | tf_op jit(solution)/shard_map/pallas_call | solution.py:401
  56.0 1.0 %shard_map.76 = (bf16[32,512]{1,0:T(8,128)(2,1)}, bf16[32,512]{1,0:T(8,128)(2,1)}, f32[27,32,256]{2,1,0:T(8,128)}, f32[1,32]{1,0:T(1,128)}) custom-call(bf16[32,512]{1,0:T(8,128)(2,1)S(1)} %get-tuple-element.12.act, bf16[32,512]{1,0:T(8,128)(2,1)S(1)} %get-tuple-element.13.gin, f32[27,32,256]{2,1,0:T(8,128)S(1)} %get-tuple-element.14.gw, ...), custom_call_target="tpu_custom_call" | custom-call | tf_op jit(solution)/shard_map/pallas_call | solution.py:448
